TPU v7x, 32 devices: a whole 2x2x4 slice. The times are simulated.
32 devices in a mesh: proto: 16 (over z, y, core), rows: 2 (over x).
Axes of the slice: x: 2, y: 2, z: 4, core: 2. Of those that a mesh axis runs over, the one named last changes fastest.
Arguments:
- student: float32 [2048, 384], P('rows'), may hold values from -15 to 15
- teacher: float32 [2048, 384], P('rows'), may hold values from -30 to 30
- proto_raw: float32 [384, 8192], P(None, 'proto'), may hold values from -60 to 60
- weights: float32 [2048], P('rows'), may hold values from 0.25 to 4
- mask: int32 [2048], P('rows'), may hold values from 0 to 1, as said below
Outputs:
- grad_student: float32 [2048, 384], P('rows')
- grad_proto: float32 [384, 8192], P('rows', 'proto')
Inputs may be any that keep to these rules, and one draw needn't show every extreme that they name: `mask`: row 0 is always 1.
All inputs are finite; a program needn't handle non-finite values.
Results may differ from a plain program's by a relative error of at most 0.00029.
Values sent between devices are 32-bit elements; how exact they have to be, the bound alone decides.
A program may use at most 64 MiB of HBM per device.

v0:
```python
import jax
import jax.numpy as jnp
from jax import lax
from jax.sharding import PartitionSpec as P

ITERS = 3


eps = 1e-06
teach_temp = 0.07
student_temp = 0.1


def unit_rows(values):
    scale = lax.rsqrt(jnp.sum(values * values, axis=1, keepdims=True) + eps)
    return (values * scale, scale)


def row_total(values):
    return lax.psum(jnp.sum(values, axis=1, keepdims=True), "proto")


def column_step(target, mask_float):
    return target / lax.psum(jnp.sum(target * mask_float, axis=0, keepdims=True), "rows")


def shards(student, teacher, proto_raw, weights, mask):
    highest = lax.Precision.HIGHEST
    s_n, s_scale = unit_rows(student)
    t_n, unused = unit_rows(teacher)
    c_scale = lax.rsqrt(jnp.sum(proto_raw * proto_raw, axis=0, keepdims=True) + eps)
    w_n = proto_raw * c_scale
    mask_float = mask.astype(jnp.float32)[:, None]
    cos_t = jnp.dot(t_n, w_n, precision=highest)
    cos_s = jnp.dot(s_n, w_n, precision=highest)
    target = jnp.exp(cos_t / teach_temp)
    target = target / row_total(target)
    student_exp = jnp.exp(cos_s / student_temp)
    for step in range(ITERS):
        target = column_step(target, mask_float)
        target = target / row_total(target)
    zsum = lax.psum(jnp.sum(student_exp, axis=1, keepdims=True), "proto")
    prob = student_exp / zsum
    coef = weights[:, None] * mask_float
    dcos = coef * (prob - target) / student_temp
    d_sn = lax.psum(jnp.dot(dcos, w_n.T, precision=highest), "proto")
    grad_student = (d_sn - s_n * jnp.sum(s_n * d_sn, axis=1, keepdims=True)) * s_scale
    share = w_n.shape[0] // lax.axis_size("rows")
    first = lax.axis_index("rows") * share
    d_wn = lax.psum(jnp.dot(s_n.T, dcos, precision=highest), "rows")
    whole = (d_wn - w_n * jnp.sum(w_n * d_wn, axis=0, keepdims=True)) * c_scale
    grad_proto = lax.dynamic_slice_in_dim(whole, first, share, 0)
    return (grad_student, grad_proto)


def solution(mesh):
    return jax.shard_map(
        shards,
        mesh=mesh,
        in_specs=(P("rows", None), P("rows", None), P(None, "proto"), P("rows"), P("rows")),
        out_specs=(P("rows", None), P("rows", "proto")),
        check_vma=False,
    )
```

profile of v0, /device:TPU:0, one launch (start us, length us, event | category | flops | bytes accessed | tf_op | source)
XLA Modules:
  0.0 315.4 jit_solution(7884611546582325548)
XLA Ops:
  7.2 0.0 all-reduce.6.cloned.1.call-start
  7.2 1.4 multiply_reduce_fusion.5
  8.6 1.2 broadcast_multiply_fusion
  9.9 0.2 multiply_reduce_fusion.2
  10.1 3.9 %fusion.27 = (f32[1024]{0:T(1024)S(1)}, f32[1024,512]{0,1:T(8,128)S(1)}) fusion(f32[384,512]{1,0:T(8,128)S(1)} %broadcast_multiply_fusion, f32[1024,384]{1,0:T(8,128)S(1)} %copy-done.5, f32[1024]{0:T(1024)S(1)} %add_rsqrt_fusion), kind=kOutput, calls=%fused_computation.46 | convolution fusion | flops 2417359872 | bytes 4464640 | tf_op jit(solution)/shard_map/dot_general | solution.py:34
  14.0 34.9 %psum.71 = f32[1024]{0:T(1024)S(1)} all-reduce(f32[1024]{0:T(1024)S(1)} %get-tuple-element.4), channel_id=1, replica_groups=mesh['proto'=16,'rows'=2] {'proto'}, use_global_device_ids=true, to_apply=%region_6.0 | all-reduce | flops 1024 | bytes 8192 | tf_op jit(solution)/shard_map/psum | solution.py:20
  48.9 0.3 multiply_reduce_fusion
  49.2 4.9 %psum.72 = f32[512]{0:T(512)S(1)} all-reduce(f32[512]{0:T(512)S(1)} %multiply_reduce_fusion), channel_id=1, replica_groups=mesh['proto'=16,'rows'=2] {'rows'}, use_global_device_ids=true, to_apply=%region_8.0 | all-reduce | flops 512 | bytes 4096 | tf_op jit(solution)/shard_map/psum | solution.py:24
  54.2 0.4 fusion.12
  54.5 29.5 %psum.73 = f32[1024]{0:T(1024)S(1)} all-reduce(f32[1024]{0:T(1024)S(1)} %fusion.12), channel_id=1, replica_groups=mesh['proto'=16,'rows'=2] {'proto'}, use_global_device_ids=true, to_apply=%region_10.0 | all-reduce | flops 1024 | bytes 8192 | tf_op jit(solution)/shard_map/psum | solution.py:20
  84.0 0.6 fusion.14
  84.6 4.9 %psum.74 = f32[512]{0:T(512)S(1)} all-reduce(f32[512]{0:T(512)S(1)} %fusion.14), channel_id=1, replica_groups=mesh['proto'=16,'rows'=2] {'rows'}, use_global_device_ids=true, to_apply=%region_12.0 | all-reduce | flops 512 | bytes 4096 | tf_op jit(solution)/shard_map/psum | solution.py:24
  89.6 0.5 fusion.13
  90.1 29.5 %psum.75 = f32[1024]{0:T(1024)S(1)} all-reduce(f32[1024]{0:T(1024)S(1)} %fusion.13), channel_id=1, replica_groups=mesh['proto'=16,'rows'=2] {'proto'}, use_global_device_ids=true, to_apply=%region_14.0 | all-reduce | flops 1024 | bytes 8192 | tf_op jit(solution)/shard_map/psum | solution.py:20
  119.6 0.8 fusion.16
  120.3 4.9 %psum.76 = f32[512]{0:T(512)S(1)} all-reduce(f32[512]{0:T(512)S(1)} %fusion.16), channel_id=1, replica_groups=mesh['proto'=16,'rows'=2] {'rows'}, use_global_device_ids=true, to_apply=%region_16.0 | all-reduce | flops 512 | bytes 4096 | tf_op jit(solution)/shard_map/psum | solution.py:24
  125.3 0.6 fusion.15
  125.9 0.8 copy-done
  126.7 0.2 multiply_reduce_fusion.3
  126.9 5.2 %fusion.17 = (f32[1024]{0:T(1024)S(1)}, f32[1024,512]{0,1:T(8,128)}) fusion(f32[384,512]{1,0:T(8,128)S(1)} %broadcast_multiply_fusion, f32[1024,384]{1,0:T(8,128)S(1)} %copy-done, f32[1024]{0:T(1024)S(1)} %add_rsqrt_fusion.1), kind=kOutput, calls=%fused_computation.23 | convolution fusion | flops 2417359872 | bytes 4464640 | tf_op jit(solution)/shard_map/dot_general | solution.py:35
  132.1 30.2 %all-reduce = (f32[1024]{0:T(1024)S(1)}, f32[1024]{0:T(1024)S(1)}) all-reduce(f32[1024]{0:T(1024)S(1)} %fusion.15, f32[1024]{0:T(1024)S(1)} %get-tuple-element.6), channel_id=1, replica_groups=mesh['proto'=16,'rows'=2] {'proto'}, use_global_device_ids=true, to_apply=%region_18.0 | all-reduce | flops 2048 | bytes 16384 | tf_op jit(solution)/shard_map/psum | solution.py:20
  162.3 2.8 multiply_multiply_fusion.1
  165.1 1.3 copy-done.3
  166.5 6.2 %fusion.19 = f32[384,512]{1,0:T(8,128)} fusion(f32[1024,512]{0,1:T(8,128)S(1)} %multiply_multiply_fusion.1, f32[1024,384]{1,0:T(8,128)S(1)} %copy-done.1, f32[1024]{0:T(1024)S(1)} %add_rsqrt_fusion.1), kind=kOutput, calls=%fused_computation.29 | convolution fusion | flops 2416312320 | bytes 4460544 | tf_op jit(solution)/shard_map/dot_general | solution.py:50
  172.7 0.3 all-reduce.4.cloned.1.call-start
  173.0 9.4 %fusion.28 = f32[1024,384]{1,0:T(8,128)} fusion(f32[1024,512]{0,1:T(8,128)} %copy-done.3, f32[384,512]{1,0:T(8,128)S(1)} %broadcast_multiply_fusion), kind=kOutput, calls=%fused_computation.47 | convolution fusion | flops 2415919104 | bytes 4456448 | tf_op jit(solution)/shard_map/dot_general | solution.py:46
  182.4 22.1 %all-reduce.6.cloned.1.call-done = f32[384,512]{1,0:T(8,128)} async-done(((f32[384,512]{1,0:T(8,128)}), f32[384,512]{1,0:T(8,128)}) %all-reduce.6.cloned.1.call-update) | async-done | bytes 786448 | tf_op jit(solution)/shard_map/psum | solution.py:50
  204.5 1.5 multiply_reduce_fusion.4
  206.0 98.3 %all-reduce.4.cloned.1.call-done = f32[1024,384]{1,0:T(8,128)} async-done(((f32[1024,384]{1,0:T(8,128)}), f32[1024,384]{1,0:T(8,128)}) %all-reduce.4.cloned.1.call-update) | async-done | bytes 1572880 | tf_op jit(solution)/shard_map/psum | solution.py:46
  304.3 1.9 multiply_reduce_fusion.1
  306.2 1.5 subtract_multiply_fusion
  307.7 0.8 fusion.26
  (25 shorter events, 0.1 us)
Async XLA Ops:
  7.2 2.7 copy-start.4
  7.2 197.3 %all-reduce.6.cloned.1.call-start = ((), (), s32[]{:S(2)}) async-start(), calls=%async_computation.1 | async-start | bytes 1572864 | tf_op jit(solution)/shard_map/psum | solution.py:50
  7.2 2.9 copy-start.5
  10.1 38.8 %copy-start.8 = (s32[1024]{0:T(1024)S(1)}, s32[1024]{0:T(1024)}, u32[]{:S(2)}) copy-start(s32[1024]{0:T(1024)} %param.9) | copy-start | bytes 12292
  125.3 1.4 copy-start
  126.9 5.2 %copy-start.9 = (f32[1024]{0:T(1024)S(1)}, f32[1024]{0:T(1024)}, u32[]{:S(2)}) copy-start(f32[1024]{0:T(1024)} %param.8) | copy-start | bytes 12292
  162.3 4.2 %copy-start.1 = (f32[1024,384]{1,0:T(8,128)S(1)}, f32[1024,384]{1,0:T(8,128)}, u32[]{:S(2)}) copy-start(f32[1024,384]{1,0:T(8,128)} %param.5) | copy-start | bytes 4718596
  165.1 1.4 copy-start.3
  172.7 131.6 %all-reduce.4.cloned.1.call-start = ((), (), s32[]{:S(2)}) async-start(), calls=%async_computation | async-start | bytes 3145728 | tf_op jit(solution)/shard_map/psum | solution.py:46
  182.4 121.9 %copy-start.2 = (f32[1024,384]{1,0:T(8,128)S(1)}, f32[1024,384]{1,0:T(8,128)}, u32[]{:S(2)}) copy-start(f32[1024,384]{1,0:T(8,128)} %param.5) | copy-start | bytes 4718596
  304.3 1.9 copy-start.6
  306.2 1.5 copy-start.7
Sparse Core Ops, SparseCore 0:
  172.8 31.5 all-reduce.5
  208.9 95.3 all-reduce.3
where the time goes:
time: 316 us; the launch traced here: 315 us
  blocking collectives  139 us (44%)
  waiting for transfers between devices  120 us (38%)
  matrix products  24.6 us (8%)
  other arithmetic  14.7 us (5%)
  between operations  14.2 us (4%)
    psum x4, blocking collectives, row_total(): return lax.psum(jnp.sum(values, axis=1, keepdims=True), 'proto')  124 us
    psum x1, waiting for transfers between devices, shards(): d_sn = lax.psum(jnp.dot(dcos, w_n.T, precision=highest), 'proto')  98.3 us
    psum x1, waiting for transfers between devices, shards(): d_wn = lax.psum(jnp.dot(s_n.T, dcos, precision=highest), 'rows')  22.1 us
    psum x3, blocking collectives, column_step(): lax.psum(jnp.sum(target * mask_float, axis=0, keepdims=True), 'rows')  14.8 us
    dot_general x1, matrix products, shards(): d_sn = lax.psum(jnp.dot(dcos, w_n.T, precision=highest), 'proto')  9.4 us
  transfers between devices with their start and end apart: 2, of which 2 were waited for; matrix products, arithmetic and copies ran while one was open for 3% of the time, Pallas kernels for 0%

commit v1 on v0

v1 whole, which is shorter than its diff:
```python
import functools

import jax
import jax.numpy as jnp
from jax import lax
from jax.experimental import pallas as pl
from jax.experimental.pallas import tpu as pltpu
from jax.sharding import PartitionSpec as P

ITERS = 3
EPS = 1e-06
TEACH = 1.0 / 0.07
STUDENT = 1.0 / 0.1
TILES = 4
LANES = 128
f32 = jnp.float32
bf16 = jnp.bfloat16
MESH = pl.DeviceIdType.MESH


def make_levels(n):
    if n % 2:
        return [(n, 1)]
    rest = n // 2
    outer = 4 if rest == 8 else 8
    while rest % outer:
        outer //= 2
    mid = rest // outer
    levels = [(2, 1), (mid, 2), (outer, 2 * mid)]
    return [lv for lv in levels if lv[0] > 1]


def split(x):
    hi = x.astype(bf16)
    return hi, (x - hi.astype(f32)).astype(bf16)


def dot(a, b):
    return jnp.dot(a, b, preferred_element_type=f32)


def dot_t(a, b):
    return lax.dot_general(a, b, (((1,), (1,)), ((), ())), preferred_element_type=f32)


def kernel(n, nr, chunks, block, orders, student, teacher, proto, weights, mask, gs, gp, *scratch):
    (wn, cs, w_hi, w_lo, lhs, kt, et, s_hi, s_lo, d_hi, d_lo, c128, rs_out, rs_in, cp_out, cp_in,
     acc, dw, dw_in, cd_out, cd_in,
     rs_ss, rs_rs, cp_ss, cp_rs, dw_ss, dw_rs, cd_ss, cd_rs, red_ss, red_rs, gat_ss, gat_rs) = scratch[:33]
    red_in = scratch[33:]
    nl = len(orders[0])
    dim, protos = proto.shape
    rows = student.shape[0]
    tile = rows // TILES
    share = dim // nr
    me = lax.axis_index("proto")
    mx = lax.axis_index("rows")

    def peer(k):
        return {"proto": lax.rem(me + k, n)}

    def rpeer(k):
        return {"rows": lax.rem(mx + k, nr)}

    barrier = pltpu.get_barrier_semaphore()

    def greet(k, carry):
        pl.semaphore_signal(barrier, inc=1, device_id=peer(k), device_id_type=MESH)
        return carry

    lax.fori_loop(1, n, greet, 0)
    for k in range(1, nr):
        pl.semaphore_signal(barrier, inc=1, device_id=rpeer(k), device_id_type=MESH)

    for i in range(protos // LANES):
        cols = slice(i * LANES, (i + 1) * LANES)
        w = proto[:, cols]
        scale = lax.rsqrt(jnp.sum(w * w, axis=0, keepdims=True) + EPS)
        w = w * scale
        cs[:, cols] = scale
        wn[:, cols] = w
        hi, lo = split(w)
        w_hi[:, cols] = hi
        w_lo[:, cols] = lo
        hi, lo = split(w.T)
        lhs[cols, 0:dim] = hi
        lhs[cols, dim : 2 * dim] = hi
        lhs[cols, 2 * dim : 3 * dim] = lo

    def unit(x):
        return x * lax.rsqrt(jnp.sum(x * x, axis=1, keepdims=True) + EPS)

    def teach(i, carry):
        at = pl.ds(pl.multiple_of(i * tile, tile), tile)
        hi, lo = split(unit(teacher[at, :]))
        cos = dot_t(lhs[...], jnp.concatenate([hi, lo, hi], axis=1))
        q = jnp.exp(cos * TEACH)
        kt[:, at] = q
        rs_out[0, :, at] = jnp.sum(q, axis=0, keepdims=True)
        return carry

    def study(i, carry):
        at = pl.ds(pl.multiple_of(i * tile, tile), tile)
        hi, lo = split(unit(student[at, :]))
        s_hi[at, :] = hi
        s_lo[at, :] = lo
        cos = dot_t(lhs[...], jnp.concatenate([hi, lo, hi], axis=1))
        q = jnp.exp(cos * STUDENT)
        et[:, at] = q
        rs_out[ITERS + 1, :, at] = jnp.sum(q, axis=0, keepdims=True)
        return carry

    def row_start(rd):
        def send(k, carry):
            pltpu.make_async_remote_copy(
                rs_out.at[rd], rs_in.at[rd, k - 1], rs_ss.at[rd], rs_rs.at[rd],
                device_id=peer(k), device_id_type=MESH).start()
            return carry

        lax.fori_loop(1, n, send, 0)

    def row_total(rd):
        pltpu.make_async_copy(rs_in.at[rd], rs_in.at[rd], rs_rs.at[rd]).wait()
        return rs_out[rd] + jnp.sum(rs_in[rd], axis=0)

    def col_copy(it, k):
        return pltpu.make_async_remote_copy(
            cp_out.at[it], cp_in.at[it, k - 1], cp_ss.at[it, k - 1], cp_rs.at[it, k - 1],
            device_id=rpeer(k), device_id_type=MESH)

    lax.fori_loop(0, TILES, teach, 0)
    pl.semaphore_wait(barrier, n - 1 + nr - 1)
    row_start(0)
    lax.fori_loop(0, TILES, study, 0)
    row_start(ITERS + 1)
    mask_f = mask[...].astype(f32)
    r = 1.0 / row_total(0)
    for it in range(ITERS):
        rm = r * mask_f
        for i in range(protos // LANES):
            at = slice(i * LANES, (i + 1) * LANES)
            part = kt[at, 0:LANES] * rm[:, 0:LANES]
            for j in range(1, rows // LANES):
                lane = slice(j * LANES, (j + 1) * LANES)
                part = part + kt[at, lane] * rm[:, lane]
            cp_out[it, :, at] = jnp.sum(part.T, axis=0, keepdims=True)
        for k in range(1, nr):
            col_copy(it, k).start()
        total = cp_out[it]
        for k in range(1, nr):
            col_copy(it, k).wait_recv()
            total = total + cp_in[it, k - 1]
        c = 1.0 / total
        for i in range(protos // LANES):
            at = slice(i * LANES, (i + 1) * LANES)
            c128[at, :] = jnp.broadcast_to(c[:, at], (LANES, LANES)).T
        for j in range(rows // LANES):
            lane = slice(j * LANES, (j + 1) * LANES)
            rs_out[it + 1, :, lane] = jnp.sum(kt[:, lane] * c128[...], axis=0, keepdims=True)
        row_start(it + 1)
        r = 1.0 / row_total(it + 1)
    zsum = row_total(ITERS + 1)
    coef = weights[...] * mask_f * STUDENT
    pa = coef / zsum
    pb = coef * r

    state = [(0, block)] * chunks

    def place(g, l):
        size, stride = orders[g][l]
        return size, stride, lax.rem(me // stride, size)

    def red_copy(g, l, k):
        size, stride, mine = place(g, l)
        off, ln = state[g]
        sub = ln // size
        to = lax.rem(mine + k, size)
        return pltpu.make_async_remote_copy(
            acc.at[g, pl.ds(pl.multiple_of(off + to * sub, 8), sub)], red_in[g * nl + l].at[k - 1],
            red_ss.at[g, l, k - 1], red_rs.at[g, l, k - 1],
            device_id={"proto": me + (to - mine) * stride}, device_id_type=MESH)

    def red_start(g, l):
        for k in range(1, orders[g][l][0]):
            red_copy(g, l, k).start()

    def red_finish(g, l):
        size, stride, mine = place(g, l)
        off, ln = state[g]
        sub = ln // size
        for k in range(1, size):
            red_copy(g, l, k).wait_recv()
        off = pl.multiple_of(off + mine * sub, 8)
        at = pl.ds(off, sub)
        total = acc[g, at, :]
        for k in range(1, size):
            total = total + red_in[g * nl + l][k - 1]
        state[g] = (off, sub)
        if l < nl - 1:
            acc[g, at, :] = total
            return
        first = g * block + off
        first = pl.multiple_of(jnp.minimum(first, rows - sub), 8)
        st = student[pl.ds(first, sub), :]
        scale = lax.rsqrt(jnp.sum(st * st, axis=1, keepdims=True) + EPS)
        st = st * scale
        gs[g, at, :] = (total - st * jnp.sum(st * total, axis=1, keepdims=True)) * scale

    def gat_copy(g, l, k):
        size, stride, mine = place(g, l)
        off, ln = state[g]
        to = lax.rem(mine + k, size)
        at = pl.ds(pl.multiple_of(off, 8), ln)
        return pltpu.make_async_remote_copy(
            gs.at[g, at], gs.at[g, at], gat_ss.at[g, l, k - 1], gat_rs.at[g, l, k - 1],
            device_id={"proto": me + (to - mine) * stride}, device_id_type=MESH)

    def gat_start(g, l):
        for k in range(1, orders[g][l][0]):
            gat_copy(g, l, k).start()

    def gat_finish(g, l):
        size, stride, mine = place(g, l)
        off, ln = state[g]
        for k in range(1, size):
            gat_copy(g, l, k).wait_recv()
        for k in range(1, size):
            gat_copy(g, l, k).wait_send()
        state[g] = (off - mine * ln, ln * size)

    def stage(g, s):
        if s > 0:
            if s <= nl:
                red_finish(g, s - 1)
            else:
                gat_finish(g, 2 * nl - s)
        if s < nl:
            red_start(g, s)
        elif s < 2 * nl:
            gat_start(g, 2 * nl - 1 - s)

    def student_tile(i):
        at = slice(i * tile, (i + 1) * tile)
        cc = jnp.concatenate([c128[...]] * (tile // LANES), axis=1)
        hi, lo = split(et[:, at] * pa[:, at] - kt[:, at] * cc * pb[:, at])
        d_hi[:, at] = hi
        d_lo[:, at] = lo
        part = dot(w_hi[...], hi) + dot(w_lo[...], hi) + dot(w_hi[...], lo)
        g, first = divmod(i * tile, block)
        acc[g, first : first + tile, :] = part.T

    def dw_copy(k):
        to = lax.rem(mx + k, nr)
        at = pl.ds(pl.multiple_of(to * share, 8), share)
        return pltpu.make_async_remote_copy(
            dw.at[at], dw_in.at[k - 1], dw_ss.at[k - 1], dw_rs.at[k - 1],
            device_id={"rows": to}, device_id_type=MESH)

    def cd_copy(k):
        return pltpu.make_async_remote_copy(
            cd_out, cd_in.at[k - 1], cd_ss.at[k - 1], cd_rs.at[k - 1],
            device_id=rpeer(k), device_id_type=MESH)

    def proto_block(i):
        at = slice(i * LANES, (i + 1) * LANES)
        hi = d_hi[at, :]
        part = (dot(hi, s_hi[...]) + dot(hi, s_lo[...]) + dot(d_lo[at, :], s_hi[...])).T
        dw[:, at] = part
        cd_out[:, at] = jnp.sum(part * wn[:, at], axis=0, keepdims=True)

    if chunks * block > rows:
        acc[chunks - 1, pl.ds(rows - (chunks - 1) * block, chunks * block - rows), :] = jnp.zeros(
            (chunks * block - rows, dim), f32)
    per = TILES // chunks
    begun = []
    for i in range(TILES):
        student_tile(i)
        if (i + 1) % per == 0:
            stage(i // per, 0)
    for i in range(protos // LANES):
        proto_block(i)
    for k in range(1, nr):
        dw_copy(k).start()
        cd_copy(k).start()
    for t in range(1, 2 * nl + chunks):
        for g in range(chunks):
            if 1 <= t - g <= 2 * nl:
                stage(g, t - g)

    for k in range(1, nr):
        cd_copy(k).wait_recv()
        dw_copy(k).wait_recv()
    mine = pl.ds(pl.multiple_of(mx * share, 8), share)
    total = dw[mine, :]
    along = cd_out[...]
    for k in range(1, nr):
        total = total + dw_in[k - 1]
        along = along + cd_in[k - 1]
    gp[...] = (total - wn[mine, :] * along) * cs[...]

    for k in range(1, nr):
        cd_copy(k).wait_send()
        dw_copy(k).wait_send()
        for it in range(ITERS):
            col_copy(it, k).wait_send()
    for g in range(chunks):
        state[g] = (0, block)
        for l in range(nl):
            for k in range(1, orders[g][l][0]):
                red_copy(g, l, k).wait_send()
            state[g] = (0, state[g][1] // orders[g][l][0])
    for rd in range(ITERS + 2):
        pltpu.make_async_copy(rs_in.at[rd], rs_in.at[rd], rs_ss.at[rd]).wait()


def shards(n, nr, student, teacher, proto_raw, weights, mask):
    rows, dim = student.shape
    protos = proto_raw.shape[1]
    share = dim // nr
    levels = make_levels(n)
    nl = len(levels)
    chunks = TILES if rows % (TILES * n * 8) == 0 else 1
    piece = -(-rows // (chunks * n * 8)) * 8
    block = piece * n
    orders = [levels for g in range(chunks)]
    biggest = max(size for size, stride in levels)
    red_in = []
    for order in orders:
        ln = block
        for size, stride in order:
            ln //= size
            red_in.append(pltpu.VMEM((size - 1, ln, dim), f32))
    dma = pltpu.SemaphoreType.DMA
    rounds = ITERS + 2
    scratch = [
        pltpu.VMEM((dim, protos), f32),
        pltpu.VMEM((1, protos), f32),
        pltpu.VMEM((dim, protos), bf16),
        pltpu.VMEM((dim, protos), bf16),
        pltpu.VMEM((protos, 3 * dim), bf16),
        pltpu.VMEM((protos, rows), f32),
        pltpu.VMEM((protos, rows), f32),
        pltpu.VMEM((rows, dim), bf16),
        pltpu.VMEM((rows, dim), bf16),
        pltpu.VMEM((protos, rows), bf16),
        pltpu.VMEM((protos, rows), bf16),
        pltpu.VMEM((protos, LANES), f32),
        pltpu.VMEM((rounds, 1, rows), f32),
        pltpu.VMEM((rounds, n - 1, 1, rows), f32),
        pltpu.VMEM((ITERS, 1, protos), f32),
        pltpu.VMEM((ITERS, nr - 1, 1, protos), f32),
        pltpu.VMEM((chunks, block, dim), f32),
        pltpu.VMEM((dim, protos), f32),
        pltpu.VMEM((nr - 1, share, protos), f32),
        pltpu.VMEM((1, protos), f32),
        pltpu.VMEM((nr - 1, 1, protos), f32),
        dma((rounds,)), dma((rounds,)),
        dma((ITERS, nr - 1)), dma((ITERS, nr - 1)),
        dma((nr - 1,)), dma((nr - 1,)), dma((nr - 1,)), dma((nr - 1,)),
        dma((chunks, nl, biggest - 1)), dma((chunks, nl, biggest - 1)),
        dma((chunks, nl, biggest - 1)), dma((chunks, nl, biggest - 1)),
    ] + red_in
    vmem = pl.BlockSpec(memory_space=pltpu.VMEM)
    grad_student, grad_proto = pl.pallas_call(
        functools.partial(kernel, n, nr, chunks, block, orders),
        out_shape=(
            jax.ShapeDtypeStruct((chunks, block, dim), f32),
            jax.ShapeDtypeStruct((share, protos), f32),
        ),
        in_specs=[vmem] * 5,
        out_specs=(vmem, vmem),
        scratch_shapes=scratch,
        compiler_params=pltpu.CompilerParams(
            collective_id=0, has_side_effects=True, vmem_limit_bytes=56 * 1024 * 1024),
    )(student, teacher, proto_raw, weights.reshape(1, rows), mask.reshape(1, rows))
    return grad_student.reshape(chunks * block, dim)[:rows], grad_proto


def solution(mesh):
    n, nr = mesh.shape["proto"], mesh.shape["rows"]
    return jax.shard_map(
        functools.partial(shards, n, nr),
        mesh=mesh,
        in_specs=(P("rows", None), P("rows", None), P(None, "proto"), P("rows"), P("rows")),
        out_specs=(P("rows", None), P("rows", "proto")),
        check_vma=False,
    )
```

time: 316 us -> 80.3 us (0.25)
  blocking collectives: 139 us -> 0 us
  waiting for transfers between devices: 120 us -> 0 us
  Pallas kernels: 0 us -> 76 us
  matrix products: 24.6 us -> 0 us
  other arithmetic: 14.7 us -> 0 us
  between operations: 14.2 us -> 0.65 us
    psum x7 -> x0, blocking collectives: 139 us -> none  [the longest x4 124 us: row_total(): return lax.psum(jnp.sum(values, axis=1, keepdims=True), 'proto')]
    psum x2 -> x0, waiting for transfers between devices: 120 us -> none  [the longest x1 98.3 us: shards(): d_sn = lax.psum(jnp.dot(dcos, w_n.T, precision=highest), 'proto')]
    pallas_call x0 -> x1, Pallas kernels: none -> 76 us  [shards(): pl.pallas_call(functools.partial(kernel, n, nr, chunks, block, orders), o...]
    dot_general x4 -> x0, matrix products: 24.6 us -> none  [the longest x1 9.4 us: shards(): d_sn = lax.psum(jnp.dot(dcos, w_n.T, precision=highest), 'proto')]
    reduce_sum x11 -> x0, other arithmetic: 8.33 us -> none  [the longest x1 1.9 us: shards(): jnp.sum(s_n * d_sn, axis=1, keepdims=True)]
    mul x4 -> x0, other arithmetic: 3.57 us -> none  [the longest x1 1.52 us: shards(): (d_sn - s_n * jnp.sum(s_n * d_sn, axis=1, keepdims=True)) * s_scale]
  transfers between devices with their start and end apart: 2 -> 0, of which waited for: 2 -> 0; matrix products, arithmetic and copies ran while one was open for 3% -> 0% of each run, Pallas kernels for 0% -> 0%
where the time goes in v1:
time: 80.3 us; the launch traced here: 80.1 us
  Pallas kernels  76 us (95%)
  local copies, waits for them, and re-layouts  3.45 us (4%)
    pallas_call x1, Pallas kernels, shards(): pl.pallas_call(functools.partial(kernel, n, nr, chunks, block, orders), o...  76 us
    unnamed x4, local copies, waits for them, and re-layouts  3.45 us

profile of v1, /device:TPU:0, one launch (start us, length us, event | category | flops | bytes accessed | tf_op | source)
XLA Modules:
  0.0 80.1 jit_solution(6354473062146171833)
XLA Ops:
  0.6 76.0 %shard_map.68 = (f32[4,256,384]{2,1,0:T(8,128)}, f32[192,512]{1,0:T(8,128)}) custom-call(f32[1024,384]{1,0:T(8,128)} %student.1, f32[1024,384]{1,0:T(8,128)} %teacher.1, f32[384,512]{1,0:T(8,128)} %proto.1, f32[1,1024]{1,0:T(1,128)} %bitcast.4, s32[1,1024]{1,0:T(1,128)} %bitcast.5), custom_call_target="tpu_custom_call" | custom-call | tf_op jit(solution)/shard_map/pallas_call | solution.py:364
  76.6 0.0 copy-start
  76.6 2.7 %copy.9 = f32[1024,384]{1,0:T(8,128)} copy(f32[1024,384]{1,0:T(8,128)} %bitcast.3) | data formatting | bytes 3145728
  79.3 0.0 copy-done
  79.4 0.7 copy.10
Async XLA Ops:
  76.6 2.7 %copy-start = (f32[192,512]{1,0:T(8,128)S(1)}, f32[192,512]{1,0:T(8,128)}, u32[]{:S(2)}) copy-start(f32[192,512]{1,0:T(8,128)} %get-tuple-element.9) | copy-start | bytes 1179652

commit v2 on v1

--- a/solution.py
+++ b/solution.py
@@ -8,6 +8,8 @@
 from jax.sharding import PartitionSpec as P
 
 ITERS = 3
+CHUNKS = 2
+FILLS = (2, 1, 1, 1, 1, 1, 1)
 EPS = 1e-06
 TEACH = 1.0 / 0.07
 STUDENT = 1.0 / 0.1
@@ -45,9 +47,9 @@
 
 def kernel(n, nr, chunks, block, orders, student, teacher, proto, weights, mask, gs, gp, *scratch):
     (wn, cs, w_hi, w_lo, lhs, kt, et, s_hi, s_lo, d_hi, d_lo, c128, rs_out, rs_in, cp_out, cp_in,
-     acc, dw, dw_in, cd_out, cd_in,
-     rs_ss, rs_rs, cp_ss, cp_rs, dw_ss, dw_rs, cd_ss, cd_rs, red_ss, red_rs, gat_ss, gat_rs) = scratch[:33]
-    red_in = scratch[33:]
+     acc, dw, dw_in, cd_out, cd_in, pe,
+     rs_ss, rs_rs, cp_ss, cp_rs, dw_ss, dw_rs, cd_ss, cd_rs, red_ss, red_rs, gat_ss, gat_rs) = scratch[:34]
+    red_in = scratch[34:]
     nl = len(orders[0])
     dim, protos = proto.shape
     rows = student.shape[0]
@@ -131,8 +133,26 @@
     lax.fori_loop(0, TILES, teach, 0)
     pl.semaphore_wait(barrier, n - 1 + nr - 1)
     row_start(0)
-    lax.fori_loop(0, TILES, study, 0)
-    row_start(ITERS + 1)
+    def project(which, i, q):
+        at = slice(i * tile, (i + 1) * tile)
+        hi, lo = split(q)
+        pe[which, :, at] = dot(w_hi[...], hi) + dot(w_lo[...], hi) + dot(w_hi[...], lo)
+
+    def project_e(i):
+        project(0, i, et[:, i * tile : (i + 1) * tile])
+
+    def study_at(i):
+        study(i, 0)
+
+    todo = [functools.partial(study_at, i) for i in range(TILES)]
+    todo.append(lambda: row_start(ITERS + 1))
+    todo += [functools.partial(project_e, i) for i in range(TILES)]
+
+    def fill(count):
+        for step in range(min(count, len(todo))):
+            todo.pop(0)()
+
+    fill(FILLS[0])
     mask_f = mask[...].astype(f32)
     r = 1.0 / row_total(0)
     for it in range(ITERS):
@@ -146,6 +166,7 @@
             cp_out[it, :, at] = jnp.sum(part.T, axis=0, keepdims=True)
         for k in range(1, nr):
             col_copy(it, k).start()
+        fill(FILLS[1 + 2 * it])
         total = cp_out[it]
         for k in range(1, nr):
             col_copy(it, k).wait_recv()
@@ -158,6 +179,15 @@
             lane = slice(j * LANES, (j + 1) * LANES)
             rs_out[it + 1, :, lane] = jnp.sum(kt[:, lane] * c128[...], axis=0, keepdims=True)
         row_start(it + 1)
+        fill(FILLS[2 + 2 * it])
+        if it == ITERS - 1:
+            fill(len(todo))
+            for i in range(TILES):
+                at = slice(i * tile, (i + 1) * tile)
+                cc = jnp.concatenate([c128[...]] * (tile // LANES), axis=1)
+                q = kt[:, at] * cc
+                kt[:, at] = q
+                project(1, i, q)
         r = 1.0 / row_total(it + 1)
     zsum = row_total(ITERS + 1)
     coef = weights[...] * mask_f * STUDENT
@@ -241,13 +271,17 @@
 
     def student_tile(i):
         at = slice(i * tile, (i + 1) * tile)
-        cc = jnp.concatenate([c128[...]] * (tile // LANES), axis=1)
-        hi, lo = split(et[:, at] * pa[:, at] - kt[:, at] * cc * pb[:, at])
+        part = (pe[0, :, at] * pa[:, at] - pe[1, :, at] * pb[:, at]).T
+        for j in range(0, tile, min(tile, block)):
+            g, first = divmod(i * tile + j, block)
+            size = min(tile, block)
+            acc[g, first : first + size, :] = part[j : j + size]
+
+    def dcos_tile(i):
+        at = slice(i * tile, (i + 1) * tile)
+        hi, lo = split(et[:, at] * pa[:, at] - kt[:, at] * pb[:, at])
         d_hi[:, at] = hi
         d_lo[:, at] = lo
-        part = dot(w_hi[...], hi) + dot(w_lo[...], hi) + dot(w_hi[...], lo)
-        g, first = divmod(i * tile, block)
-        acc[g, first : first + tile, :] = part.T
 
     def dw_copy(k):
         to = lax.rem(mx + k, nr)
@@ -271,12 +305,14 @@
     if chunks * block > rows:
         acc[chunks - 1, pl.ds(rows - (chunks - 1) * block, chunks * block - rows), :] = jnp.zeros(
             (chunks * block - rows, dim), f32)
-    per = TILES // chunks
-    begun = []
+    begun = 0
     for i in range(TILES):
         student_tile(i)
-        if (i + 1) % per == 0:
-            stage(i // per, 0)
+        while (begun + 1) * block <= (i + 1) * tile or (i == TILES - 1 and begun < chunks):
+            stage(begun, 0)
+            begun += 1
+    for i in range(TILES):
+        dcos_tile(i)
     for i in range(protos // LANES):
         proto_block(i)
     for k in range(1, nr):
@@ -319,7 +355,7 @@
     share = dim // nr
     levels = make_levels(n)
     nl = len(levels)
-    chunks = TILES if rows % (TILES * n * 8) == 0 else 1
+    chunks = CHUNKS if rows % (CHUNKS * n * 8) == 0 else 1
     piece = -(-rows // (chunks * n * 8)) * 8
     block = piece * n
     orders = [levels for g in range(chunks)]
@@ -354,6 +390,7 @@
         pltpu.VMEM((nr - 1, share, protos), f32),
         pltpu.VMEM((1, protos), f32),
         pltpu.VMEM((nr - 1, 1, protos), f32),
+        pltpu.VMEM((2, dim, rows), f32),
         dma((rounds,)), dma((rounds,)),
         dma((ITERS, nr - 1)), dma((ITERS, nr - 1)),
         dma((nr - 1,)), dma((nr - 1,)), dma((nr - 1,)), dma((nr - 1,)),

time: 80.3 us -> 74.9 us (0.933)
  Pallas kernels: 76 us -> 70.6 us
    pallas_call x1, Pallas kernels: 76 us -> 70.6 us  [shards(): pl.pallas_call(functools.partial(kernel, n, nr, chunks, block, orders), o...]
where the time goes in v2:
time: 74.9 us; the launch traced here: 74.7 us
  Pallas kernels  70.6 us (94%)
  local copies, waits for them, and re-layouts  3.45 us (5%)
    pallas_call x1, Pallas kernels, shards(): pl.pallas_call(functools.partial(kernel, n, nr, chunks, block, orders), o...  70.6 us
    unnamed x4, local copies, waits for them, and re-layouts  3.45 us

profile of v2, /device:TPU:0, one launch (start us, length us, event | category | flops | bytes accessed | tf_op | source)
XLA Modules:
  0.0 74.7 jit_solution(10008708578317924401)
XLA Ops:
  0.6 70.6 %shard_map.68 = (f32[2,512,384]{2,1,0:T(8,128)}, f32[192,512]{1,0:T(8,128)}) custom-call(f32[1024,384]{1,0:T(8,128)} %student.1, f32[1024,384]{1,0:T(8,128)} %teacher.1, f32[384,512]{1,0:T(8,128)} %proto.1, f32[1,1024]{1,0:T(1,128)} %bitcast.4, s32[1,1024]{1,0:T(1,128)} %bitcast.5), custom_call_target="tpu_custom_call" | custom-call | tf_op jit(solution)/shard_map/pallas_call | solution.py:401
  71.3 0.0 copy-start
  71.3 2.7 %copy.9 = f32[1024,384]{1,0:T(8,128)} copy(f32[1024,384]{1,0:T(8,128)} %bitcast.3) | data formatting | bytes 3145728
  74.0 0.0 copy-done
  74.0 0.7 copy.10
Async XLA Ops:
  71.3 2.7 %copy-start = (f32[192,512]{1,0:T(8,128)S(1)}, f32[192,512]{1,0:T(8,128)}, u32[]{:S(2)}) copy-start(f32[192,512]{1,0:T(8,128)} %get-tuple-element.9) | copy-start | bytes 1179652
